TPU v7x, 128 devices: a whole 4x4x4 slice. The times are simulated.
128 devices in a mesh: section: 64 (over z, y, x_hi, core), cfg: 2 (over x_lo).
Axes of the slice: x: 4 (x_hi: 2, x_lo: 2; x = x_hi * 2 + x_lo), y: 4, z: 4, core: 2. Of those that a mesh axis runs over, the one named last changes fastest.
Arguments:
- patches: bfloat16 [64, 384, 3072], P('section', 'cfg'), may hold values from -6 to 6
- patch_index: int32 [64], replicated, may hold values from 0 to 3
- step_index: int32 [64], replicated, may hold values from 0 to 27
- counts: int32 [4], replicated, may hold values from 1 to 384, 1152 in all
- modulation: bfloat16 [64, 28, 3, 3072], P('section'), may hold values from -3 to 3
- qk_gain: float32 [64, 2, 128], P('section'), may hold values from 0.6 to 4.5
- w_qkv: bfloat16 [64, 3, 3072, 1536], P('section', None, None, 'cfg'), may hold values from -0.108253175 to 0.108253175
- w_out: bfloat16 [64, 1536, 3072], P('section', 'cfg'), may hold values from -0.15625 to 0.15625
- cache_k: bfloat16 [64, 1792, 1536], P('section', None, 'cfg'), may hold values from -6 to 6
- cache_v: bfloat16 [64, 1792, 1536], P('section', None, 'cfg'), may hold values from -6 to 6
Outputs:
- result: bfloat16 [64, 384, 3072], P('section', 'cfg')
Inputs may be any that keep to these rules, and one draw needn't show every extreme that they name: `counts`: some patch is full.
All inputs are finite; a program needn't handle non-finite values.
Results may differ from a plain program's by a relative error of at most 0.015.
Values may be sent and summed in bfloat16 or wider, within the bound.
No kernel may reach another device: no remote copies, remote signals or barrier semaphores. Data moves between devices by JAX's collectives and lax.ppermute only.
A program may use at most 192 MiB of HBM per device.

v0:
```python
import jax
import jax.numpy as jnp
from jax import lax
from jax.experimental import pallas as pl
from jax.experimental.pallas import tpu as pltpu
from jax.sharding import PartitionSpec as P

HD = 128
PATCH_TOK = 384
NPATCH = 4
TEXT = 256
SECTIONS = 64
BF16 = jnp.bfloat16
F32 = jnp.float32
VMEM = pl.BlockSpec(memory_space=pltpu.VMEM)
SMEM = pl.BlockSpec(memory_space=pltpu.SMEM)
HBM = pl.BlockSpec(memory_space=pltpu.HBM)
MIB = 1024 * 1024
QUERY_SCALE = HD ** (-0.5) * 1.4426950408889634
BLOCK = 1536
MID = (96, 96)
LAST = (64, 64, 64)


def held(array):
    return pltpu.with_memory_space_constraint(array, pltpu.VMEM)


def far(array):
    return pltpu.with_memory_space_constraint(array, pltpu.HBM)


def in_vmem(shape, dtype):
    return pltpu.VMEM(shape, dtype)


def loose(shape, dtype):
    return jax.ShapeDtypeStruct(shape, dtype)


def modulated(rows, mods):
    wide = rows.astype(F32)
    mean = jnp.mean(wide, axis=-1, keepdims=True)
    centred = wide - mean
    spread = jnp.mean(centred * centred, axis=-1, keepdims=True)
    normed = centred * lax.rsqrt(spread + 1e-06)
    return (normed * (1.0 + mods[1:2]) + mods[0:1]).astype(BF16)


def head_norm(proj, gain):
    parts = []
    for head in range(proj.shape[1] // HD):
        x = proj[:, head * HD : (head + 1) * HD]
        scale = lax.rsqrt(jnp.mean(x * x, axis=-1, keepdims=True) + 1e-06)
        parts.append((x * scale * gain).astype(BF16))
    return jnp.concatenate(parts, axis=1)


def project(hidden, weights):
    return jnp.dot(hidden, weights, preferred_element_type=F32)


def limit(mib):
    return pltpu.CompilerParams(vmem_limit_bytes=mib * MIB)


def cost(flops):
    return pl.CostEstimate(flops=int(flops), bytes_accessed=1000000, transcendentals=0)


def first_row(tick, side, patch_index, half):
    section, group = lax.axis_index("section"), lax.axis_index("cfg")
    source = lax.rem(section + SECTIONS - tick, SECTIONS)
    swapped = 0 if tick == 0 else 1 - lax.rem(section, 2)
    which = lax.rem(group + swapped + side, 2)
    return pl.multiple_of(TEXT + patch_index[source] * PATCH_TOK + which * half, 32)


def projections(hidden, gains, weights, waits, put_key, put_value, query):
    waits[0]()
    put_key(head_norm(project(hidden, weights[1]), gains[1:2]))
    waits[1]()
    put_value(project(hidden, weights[2]).astype(BF16))
    waits[2]()
    query[...] = head_norm(project(hidden, weights[0]), gains[0:1] * QUERY_SCALE)


def selected(modulation, step):
    at = lax.broadcasted_iota(jnp.int32, (modulation.shape[1], 1), 0) == step
    rows = [
        jnp.sum(jnp.where(at, modulation[i].astype(F32), 0.0), axis=0, keepdims=True)
        for i in range(modulation.shape[0])
    ]
    return jnp.concatenate(rows, axis=0)


def open_kernel(
    patch_far, step_far, rows_far, modulation_far, gains_far, w_qkv_far, w_out_far, keys_far, values_far,
    query, rows, upper, lower, mods_now, mods_next, gains, w_qkv, w_out, keys, values,
    modulation, patch_index, step_index, sems, more,
):
    pairs = [
        (patch_far, patch_index),
        (step_far, step_index),
        (gains_far, gains),
        (modulation_far, modulation),
        (rows_far, rows),
        (keys_far, keys),
        (values_far, values),
        (w_out_far, w_out),
    ]
    others = [pltpu.make_async_copy(a, b, more.at[i]) for i, (a, b) in enumerate(pairs)]
    for copy in others[:5]:
        copy.start()
    copies = [pltpu.make_async_copy(w_qkv_far.at[i], w_qkv.at[i], sems.at[i]) for i in (1, 2, 0)]
    for copy in copies + others[5:]:
        copy.start()
    section = lax.axis_index("section")
    for copy in others[:4]:
        copy.wait()
    mods = selected(modulation, step_index[section])
    mods_now[...] = mods
    mods_next[...] = selected(modulation, step_index[lax.rem(section + SECTIONS - 1, SECTIONS)])
    others[4].wait()
    upper[...] = rows[: upper.shape[0], :]
    lower[...] = rows[upper.shape[0] :, :]
    hidden = modulated(rows[...], mods)
    here = pl.ds(first_row(0, 0, patch_index, rows.shape[0]), rows.shape[0])

    def put_key(fresh):
        others[5].wait()
        keys[here, :] = fresh

    def put_value(fresh):
        others[6].wait()
        values[here, :] = fresh

    projections(hidden, gains[...], w_qkv, [c.wait for c in copies], put_key, put_value, query)
    others[7].wait()


def opening(patch_index, step_index, rows, modulation, gains, w_qkv, w_out, keys, values):
    model = rows.shape[1]
    return pl.pallas_call(
        open_kernel,
        in_specs=[HBM] * 9,
        out_specs=[VMEM] * 11,
        out_shape=[
            in_vmem((rows.shape[0], keys.shape[1]), BF16),
            in_vmem(rows.shape, BF16),
            loose((MID[0], model), BF16),
            loose((MID[1], model), BF16),
            loose((3, model), F32),
            loose((3, model), F32),
            loose(gains.shape, F32),
            in_vmem(w_qkv.shape, BF16),
            in_vmem(w_out.shape, BF16),
            in_vmem(keys.shape, BF16),
            in_vmem(values.shape, BF16),
        ],
        scratch_shapes=[
            pltpu.VMEM(modulation.shape, BF16),
            pltpu.SMEM(patch_index.shape, jnp.int32),
            pltpu.SMEM(step_index.shape, jnp.int32),
            pltpu.SemaphoreType.DMA((3,)),
            pltpu.SemaphoreType.DMA((8,)),
        ],
        compiler_params=limit(16),
        cost_estimate=cost(2 * w_qkv.size * 256),
        name="opening",
    )(*map(far, (patch_index, step_index, rows, modulation, gains, w_qkv, w_out, keys, values)))


def qkv(tick, side, patch_index, pairs, mods, gains, w_qkv, keys, values):
    count, width = sum(p[0].shape[0] for p in pairs), keys.shape[1]
    n = sum(map(len, pairs))

    def kernel(patch_index, *refs):
        parts, (mods, gains, w_qkv, _, _) = refs[:n], refs[n : n + 5]
        query, keys, values = refs[n + 5 :]
        rows, place = [], 0
        for p in pairs:
            one, *two = [ref[...] for ref in parts[place : place + len(p)]]
            rows.append(one + jnp.concatenate(two, axis=0) if two else one)
            place += len(p)
        hidden = modulated(rows[0] if len(pairs) == 1 else jnp.concatenate(rows, axis=0), mods[...])
        here = pl.ds(first_row(tick, side, patch_index, count), count)

        def put_key(fresh):
            keys[here, :] = fresh

        def put_value(fresh):
            values[here, :] = fresh

        none = [lambda: None] * 3
        projections(hidden, gains[...], w_qkv, none, put_key, put_value, query)

    return pl.pallas_call(
        kernel,
        in_specs=[SMEM] + [VMEM] * (n + 5),
        out_specs=[VMEM] * 3,
        out_shape=[in_vmem((count, width), BF16), in_vmem(keys.shape, BF16), in_vmem(values.shape, BF16)],
        input_output_aliases={n + 4: 1, n + 5: 2},
        compiler_params=limit(16),
        cost_estimate=cost(2 * w_qkv.size * 256),
        name="qkv",
    )(patch_index, *(a for p in pairs for a in p), mods, gains, held(w_qkv), held(keys), held(values))


def attended(query, keys, values, counts):
    total = keys.shape[0]
    place = lax.broadcasted_iota(jnp.int32, (1, total), 1)
    valid = place < TEXT
    for patch in range(NPATCH):
        begin = TEXT + patch * PATCH_TOK
        valid |= (place >= begin) & (place < begin + counts[patch])
    bias = jnp.where(valid, 0.0, -1e30)
    ones = jnp.ones((total, HD), BF16)
    outs = []
    for head in range(keys.shape[1] // HD):
        cols = slice(head * HD, (head + 1) * HD)
        scores = lax.dot_general(
            query[:, cols], keys[:, cols], (((1,), (1,)), ((), ())), preferred_element_type=F32
        )
        scores = scores + bias
        expo = jnp.exp2(scores - jnp.max(scores, axis=-1, keepdims=True)).astype(BF16)
        out = project(expo, jnp.concatenate([values[:, cols], ones], axis=1))
        outs.append((out[:, :HD] / out[:, HD:]).astype(BF16))
    return jnp.concatenate(outs, axis=1)


def attend(begin, sizes, counts, query, keys, values, w_out, pieces=(), mods=None):
    count, model = sum(sizes), w_out.shape[1]
    keep = len(pieces) > 0
    n = len(pieces)

    def kernel(counts, query, keys, values, w_out, *refs):
        out, outs = refs[-1], refs[-1 - len(sizes) : -1]
        out[...] = attended(query[begin : begin + count, :], keys, values, counts)

        def columns(i, carry):
            cols = pl.ds(pl.multiple_of(i * BLOCK, BLOCK), BLOCK)
            mixed = project(out[...], w_out[:, cols])
            if keep:
                rows = jnp.concatenate([p[:, cols] for p in refs[:n]], axis=0)
                mixed = rows.astype(F32) + refs[n][2:3, cols] * mixed
            place = 0
            for ref, size in zip(outs, sizes):
                ref[:, cols] = mixed[place : place + size].astype(ref.dtype)
                place += size
            return carry

        lax.fori_loop(0, model // BLOCK, columns, 0)

    extra = (*pieces, mods) if keep else ()
    return pl.pallas_call(
        kernel,
        in_specs=[SMEM] + [VMEM] * (4 + len(extra)),
        out_specs=[VMEM] * len(sizes),
        out_shape=[in_vmem((size, model), F32 if keep else BF16) for size in sizes],
        scratch_shapes=[pltpu.VMEM((count, query.shape[1]), BF16)],
        compiler_params=limit(16),
        cost_estimate=cost(2 * 256 * query.shape[1] * (2 * keys.shape[0] + model)),
        name="attend",
    )(counts, held(query), held(keys), held(values), held(w_out), *extra)


def combine_kernel(base, received, mods, out):
    out[...] = (base[...] + mods[2:3] * received[...].astype(F32)).astype(BF16)


def combine(base, received, mods):
    return pl.pallas_call(
        combine_kernel,
        in_specs=[VMEM] * 3,
        out_specs=VMEM,
        out_shape=in_vmem(received.shape, BF16),
        compiler_params=limit(6),
        name="combine",
    )(held(base), held(received), mods)


def on_device(
    patches, patch_index, step_index, counts, modulation, qk_gain, w_qkv, w_out, cache_k, cache_v
):
    both = ("section", "cfg")
    swap = [(2 * s + c, 2 * s + 1 - c) for s in range(SECTIONS) for c in range(2)]
    shift = [
        (2 * s + c, 2 * ((s + 1) % SECTIONS) + (c if s % 2 == 0 else 1 - c))
        for s in range(SECTIONS)
        for c in range(2)
    ]

    def exchange(block):
        return lax.ppermute(block, both, swap)

    def move(block):
        return lax.ppermute(block, both, shift)

    own = patches[0]
    early = lax.ppermute(own, both, [p for p in swap if p[0] // 2 % 2 == 0])
    query, copied, upper, lower, mods, mods_next, gains, weights, proj, keys, values = opening(
        patch_index, step_index, own, jnp.transpose(modulation[0], (1, 0, 2)), qk_gain[0], w_qkv[0],
        w_out[0], cache_k[0], cache_v[0],
    )
    late = [lax.ppermute(piece, both, [p for p in swap if p[0] // 2 % 2 == 1]) for piece in (upper, lower)]
    query_other, keys, values = qkv(
        0, 1, patch_index, [(early, *late)], mods, gains, weights, keys, values
    )
    begin = 0
    got = []
    for size in MID:
        got.append(exchange(attend(begin, (size,), counts, query_other, keys, values, proj)[0]))
        begin += size
    base = attend(0, MID, counts, query, keys, values, proj, (copied,), mods)
    own = [move(combine(b, g, mods)) for b, g in zip(base, got)]

    mods = mods_next
    other = [exchange(block) for block in own]
    query, keys, values = qkv(1, 0, patch_index, [(p,) for p in own], mods, gains, weights, keys, values)
    query_other, keys, values = qkv(1, 1, patch_index, [(p,) for p in other], mods, gains, weights, keys, values)
    one = attend(0, LAST[:1], counts, query, keys, values, proj)
    two = attend(LAST[0], LAST[1:], counts, query, keys, values, proj)
    got = [exchange(block) for block in (*one, *two)]
    base = attend(0, LAST, counts, query_other, keys, values, proj, other, mods)
    done = [move(combine(b, g, mods)) for b, g in zip(base, got)]
    return jnp.concatenate(done, axis=0)[None]


def solution(mesh):
    in_specs = (
        P("section", "cfg", None),
        P(),
        P(),
        P(),
        P("section", None, None, None),
        P("section", None, None),
        P("section", None, None, "cfg"),
        P("section", "cfg", None),
        P("section", None, "cfg"),
        P("section", None, "cfg"),
    )
    out_specs = P("section", "cfg", None)
    return jax.shard_map(
        on_device, mesh=mesh, in_specs=in_specs, out_specs=out_specs, check_vma=False
    )
```

profile of v0, /device:TPU:0, one launch (start us, length us, event | category | flops | bytes accessed | tf_op | source)
XLA Modules:
  0.0 135.5 jit_solution(16754013569967915819)
XLA Ops:
  0.0 3.5 %collective-permute-start = (bf16[192,3072]{1,0:T(8,128)(2,1)}, bf16[192,3072]{1,0:T(8,128)(2,1)S(1)}, u32[]{:S(2)}, u32[]{:S(2)}) collective-permute-start(bf16[192,3072]{1,0:T(8,128)(2,1)} %bitcast.15), channel_id=1, source_target_pairs={{0,1},{1,0},{4,5},{5,4},{8,9},{9,8},{12,13},{13,12},{16,17},{17,16... | collective-permute-start | bytes 3538952 | tf_op jit(solution)/shard_map/ppermute | solution.py:301
  3.5 8.8 %opening.1 = (bf16[192,768]{1,0:T(8,128)(2,1)S(1)}, bf16[192,3072]{1,0:T(8,128)(2,1)S(1)}, bf16[96,3072]{1,0:T(8,128)(2,1)S(1)}, bf16[96,3072]{1,0:T(8,128)(2,1)...) custom-call(s32[64]{0:T(128)} %patch_index.5, ...), custom_call_target="tpu_custom_call" | custom-call | flops 3623878656 | bytes 1000000 | tf_op jit(solution)/shard_map/opening/pallas_call | solution.py:144
  13.7 9.1 %collective-permute-done.refs_0_ = bf16[192,3072]{1,0:T(8,128)(2,1)S(1)} collective-permute-done((bf16[192,3072]{1,0:T(8,128)(2,1)}, bf16[192,3072]{1,0:T(8,128)(2,1)S(1)}, u32[]{:S(2)}, u32[]{:S(2)}) %collective-permute-start) | collective-permute-done | bytes 1179680 | tf_op jit(solution)/shard_map/ppermute | solution.py:301
  22.8 4.4 %qkv.3 = (bf16[192,768]{1,0:T(8,128)(2,1)S(1)}, bf16[1792,768]{1,0:T(8,128)(2,1)S(1)}, bf16[1792,768]{1,0:T(8,128)(2,1)S(1)}) custom-call(s32[64]{0:T(128)S(1)} %copy-done.1, bf16[192,3072]{1,0:T(8,128)(2,1)S(1)} %collective-permute-done.refs_0_, bf16[96,3072]{1,0:T(8,128)(2,1)S(1)} %collective-permute-done.1.refs_1_, ...), custom_call_target="tpu_custom_call", output_to_operand_aliasing={{1}: (7, {}), {2}: (8, {})} | custom-call | flops 3623878656 | bytes 1000000 | tf_op jit(solution)/shard_map/qkv/pallas_call | solution.py:198
  27.2 4.0 %attend.8 = bf16[96,3072]{1,0:T(8,128)(2,1)S(1)} custom-call(s32[4]{0:T(128)S(1)} %copy-done, bf16[192,768]{1,0:T(8,128)(2,1)S(1)} %get-tuple-element.45.query, bf16[1792,768]{1,0:T(8,128)(2,1)S(1)} %get-tuple-element.40.keys.refs_5_, bf16[1792,768]{1,0:T(8,128)(2,1)S(1)} %get-tuple-element.41.values.refs_6_, bf16[768,3072]{1,0:T(8,128)(2,1)S(1)} %get-tuple-element.42.w_out), custom_call_target="tpu_custom_call" | custom-call | flops 2617245696 | bytes 1000000 | tf_op jit(solution)/shard_map/attend/pallas_call | solution.py:256
  31.2 1.7 %collective-permute-start.6 = (bf16[96,3072]{1,0:T(8,128)(2,1)S(1)}, bf16[96,3072]{1,0:T(8,128)(2,1)S(1)}, u32[]{:S(2)}, u32[]{:S(2)}) collective-permute-start(bf16[96,3072]{1,0:T(8,128)(2,1)S(1)} %attend.8), channel_id=1, source_target_pairs={{0,1},{1,0},{2,3},{3,2},{4,5},{5,4},{6,7},{7,6},{8,9},{9,8},{10,11... | collective-permute-start | bytes 1769480 | tf_op jit(solution)/shard_map/ppermute | solution.py:295
  32.9 4.0 %attend.7 = bf16[96,3072]{1,0:T(8,128)(2,1)S(1)} custom-call(s32[4]{0:T(128)S(1)} %copy-done, bf16[192,768]{1,0:T(8,128)(2,1)S(1)} %get-tuple-element.45.query, bf16[1792,768]{1,0:T(8,128)(2,1)S(1)} %get-tuple-element.40.keys.refs_5_, bf16[1792,768]{1,0:T(8,128)(2,1)S(1)} %get-tuple-element.41.values.refs_6_, bf16[768,3072]{1,0:T(8,128)(2,1)S(1)} %get-tuple-element.42.w_out), custom_call_target="tpu_custom_call" | custom-call | flops 2617245696 | bytes 1000000 | tf_op jit(solution)/shard_map/attend/pallas_call | solution.py:256
  37.6 5.1 %attend.6 = (f32[96,3072]{1,0:T(8,128)S(1)}, f32[96,3072]{1,0:T(8,128)S(1)}) custom-call(s32[4]{0:T(128)S(1)} %copy-done, bf16[192,768]{1,0:T(8,128)(2,1)S(1)} %get-tuple-element.32.query, bf16[1792,768]{1,0:T(8,128)(2,1)S(1)} %get-tuple-element.40.keys.refs_5_, bf16[1792,768]{1,0:T(8,128)(2,1)S(1)} %get-tuple-element.41.values.refs_6_, ...), custom_call_target="tpu_custom_call" | custom-call | flops 2617245696 | bytes 1000000 | tf_op jit(solution)/shard_map/attend/pallas_call | solution.py:256
  42.9 11.2 %collective-permute-start.7 = (bf16[96,3072]{1,0:T(8,128)(2,1)S(1)}, bf16[96,3072]{1,0:T(8,128)(2,1)S(1)}, u32[]{:S(2)}, u32[]{:S(2)}) collective-permute-start(bf16[96,3072]{1,0:T(8,128)(2,1)S(1)} %combine.6), channel_id=1, source_target_pairs={{0,2},{1,3},{2,5},{3,4},{4,6},{5,7},{6,9},{7,8},{8,10},{9,11},{10,... | collective-permute-start | bytes 1769480 | tf_op jit(solution)/shard_map/ppermute | solution.py:298
  54.3 6.1 %collective-permute-start.4 = (bf16[96,3072]{1,0:T(8,128)(2,1)S(1)}, bf16[96,3072]{1,0:T(8,128)(2,1)S(1)}, u32[]{:S(2)}, u32[]{:S(2)}) collective-permute-start(bf16[96,3072]{1,0:T(8,128)(2,1)S(1)} %combine.5), channel_id=1, source_target_pairs={{0,2},{1,3},{2,5},{3,4},{4,6},{5,7},{6,9},{7,8},{8,10},{9,11},{10,... | collective-permute-start | bytes 1769480 | tf_op jit(solution)/shard_map/ppermute | solution.py:298
  60.4 9.5 %collective-permute-done.7.refs_1_ = bf16[96,3072]{1,0:T(8,128)(2,1)S(1)} collective-permute-done((bf16[96,3072]{1,0:T(8,128)(2,1)S(1)}, bf16[96,3072]{1,0:T(8,128)(2,1)S(1)}, u32[]{:S(2)}, u32[]{:S(2)}) %collective-permute-start.7) | collective-permute-done | bytes 589856 | tf_op jit(solution)/shard_map/ppermute | solution.py:298
  70.1 6.4 %collective-permute-done.4.refs_0_ = bf16[96,3072]{1,0:T(8,128)(2,1)S(1)} collective-permute-done((bf16[96,3072]{1,0:T(8,128)(2,1)S(1)}, bf16[96,3072]{1,0:T(8,128)(2,1)S(1)}, u32[]{:S(2)}, u32[]{:S(2)}) %collective-permute-start.4) | collective-permute-done | bytes 589856 | tf_op jit(solution)/shard_map/ppermute | solution.py:298
  76.7 4.3 %qkv.4 = (bf16[192,768]{1,0:T(8,128)(2,1)S(1)}, bf16[1792,768]{1,0:T(8,128)(2,1)S(1)}, bf16[1792,768]{1,0:T(8,128)(2,1)S(1)}) custom-call(s32[64]{0:T(128)S(1)} %copy-done.1, bf16[96,3072]{1,0:T(8,128)(2,1)S(1)} %collective-permute-done.4.refs_0_, bf16[96,3072]{1,0:T(8,128)(2,1)S(1)} %collective-permute-done.7.refs_1_, ...), custom_call_target="tpu_custom_call", output_to_operand_aliasing={{1}: (6, {}), {2}: (7, {})} | custom-call | flops 3623878656 | bytes 1000000 | tf_op jit(solution)/shard_map/qkv/pallas_call | solution.py:198
  82.5 6.3 %collective-permute-done.5.refs_0_ = bf16[96,3072]{1,0:T(8,128)(2,1)S(1)} collective-permute-done((bf16[96,3072]{1,0:T(8,128)(2,1)S(1)}, bf16[96,3072]{1,0:T(8,128)(2,1)S(1)}, u32[]{:S(2)}, u32[]{:S(2)}) %collective-permute-start.5) | collective-permute-done | bytes 589856 | tf_op jit(solution)/shard_map/ppermute | solution.py:295
  88.8 4.4 %qkv.5 = (bf16[192,768]{1,0:T(8,128)(2,1)S(1)}, bf16[1792,768]{1,0:T(8,128)(2,1)S(1)}, bf16[1792,768]{1,0:T(8,128)(2,1)S(1)}) custom-call(s32[64]{0:T(128)S(1)} %copy-done.1, bf16[96,3072]{1,0:T(8,128)(2,1)S(1)} %collective-permute-done.5.refs_0_, bf16[96,3072]{1,0:T(8,128)(2,1)S(1)} %collective-permute-done.8.refs_1_, ...), custom_call_target="tpu_custom_call", output_to_operand_aliasing={{1}: (6, {}), {2}: (7, {})} | custom-call | flops 3623878656 | bytes 1000000 | tf_op jit(solution)/shard_map/qkv/pallas_call | solution.py:198
  93.2 3.9 %attend.11 = (bf16[64,3072]{1,0:T(8,128)(2,1)S(1)}, bf16[64,3072]{1,0:T(8,128)(2,1)S(1)}) custom-call(s32[4]{0:T(128)S(1)} %copy-done, bf16[192,768]{1,0:T(8,128)(2,1)S(1)} %get-tuple-element.54.query, bf16[1792,768]{1,0:T(8,128)(2,1)S(1)} %get-tuple-element.51.keys, bf16[1792,768]{1,0:T(8,128)(2,1)S(1)} %get-tuple-element.52.values, ...), custom_call_target="tpu_custom_call" | custom-call | flops 2617245696 | bytes 1000000 | tf_op jit(solution)/shard_map/attend/pallas_call | solution.py:256
  99.1 4.1 %attend.10 = bf16[64,3072]{1,0:T(8,128)(2,1)S(1)} custom-call(s32[4]{0:T(128)S(1)} %copy-done, bf16[192,768]{1,0:T(8,128)(2,1)S(1)} %get-tuple-element.54.query, bf16[1792,768]{1,0:T(8,128)(2,1)S(1)} %get-tuple-element.51.keys, bf16[1792,768]{1,0:T(8,128)(2,1)S(1)} %get-tuple-element.52.values, bf16[768,3072]{1,0:T(8,128)(2,1)S(1)} %get-tuple-element.42.w_out), custom_call_target="tpu_custom_call" | custom-call | flops 2617245696 | bytes 1000000 | tf_op jit(solution)/shard_map/attend/pallas_call | solution.py:256
  103.2 1.7 %collective-permute-start.9 = (bf16[64,3072]{1,0:T(8,128)(2,1)S(1)}, bf16[64,3072]{1,0:T(8,128)(2,1)S(1)}, u32[]{:S(2)}, u32[]{:S(2)}) collective-permute-start(bf16[64,3072]{1,0:T(8,128)(2,1)S(1)} %attend.10), channel_id=1, source_target_pairs={{0,1},{1,0},{2,3},{3,2},{4,5},{5,4},{6,7},{7,6},{8,9},{9,8},{10,11... | collective-permute-start | bytes 1179656 | tf_op jit(solution)/shard_map/ppermute | solution.py:295
  105.0 5.1 %attend.9 = (f32[64,3072]{1,0:T(8,128)S(1)}, f32[64,3072]{1,0:T(8,128)S(1)}, f32[64,3072]{1,0:T(8,128)S(1)}) custom-call(s32[4]{0:T(128)S(1)} %copy-done, bf16[192,768]{1,0:T(8,128)(2,1)S(1)} %get-tuple-element.50.query, bf16[1792,768]{1,0:T(8,128)(2,1)S(1)} %get-tuple-element.51.keys, bf16[1792,768]{1,0:T(8,128)(2,1)S(1)} %get-tuple-element.52.values, ...), custom_call_target="tpu_custom_call" | custom-call | flops 2617245696 | bytes 1000000 | tf_op jit(solution)/shard_map/attend/pallas_call | solution.py:256
  112.7 3.3 %collective-permute-done.9.received = bf16[64,3072]{1,0:T(8,128)(2,1)S(1)} collective-permute-done((bf16[64,3072]{1,0:T(8,128)(2,1)S(1)}, bf16[64,3072]{1,0:T(8,128)(2,1)S(1)}, u32[]{:S(2)}, u32[]{:S(2)}) %collective-permute-start.9) | collective-permute-done | bytes 393248 | tf_op jit(solution)/shard_map/ppermute | solution.py:295
  116.1 4.7 %collective-permute-start.10 = (bf16[64,3072]{1,0:T(8,128)(2,1)S(1)}, bf16[64,3072]{1,0:T(8,128)(2,1)S(1)}, u32[]{:S(2)}, u32[]{:S(2)}) collective-permute-start(bf16[64,3072]{1,0:T(8,128)(2,1)S(1)} %combine.7), channel_id=1, source_target_pairs={{0,2},{1,3},{2,5},{3,4},{4,6},{5,7},{6,9},{7,8},{8,10},{9,11},{10,... | collective-permute-start | bytes 1179656 | tf_op jit(solution)/shard_map/ppermute | solution.py:298
  120.8 2.1 %collective-permute-done.12 = bf16[64,3072]{1,0:T(8,128)(2,1)S(1)} collective-permute-done((bf16[64,3072]{1,0:T(8,128)(2,1)S(1)}, bf16[64,3072]{1,0:T(8,128)(2,1)S(1)}, u32[]{:S(2)}, u32[]{:S(2)}) %collective-permute-start.12) | collective-permute-done | bytes 393248 | tf_op jit(solution)/shard_map/ppermute | solution.py:298
  122.9 4.2 %collective-permute-done.14 = bf16[64,3072]{1,0:T(8,128)(2,1)S(1)} collective-permute-done((bf16[64,3072]{1,0:T(8,128)(2,1)S(1)}, bf16[64,3072]{1,0:T(8,128)(2,1)S(1)}, u32[]{:S(2)}, u32[]{:S(2)}) %collective-permute-start.14) | collective-permute-done | bytes 393248 | tf_op jit(solution)/shard_map/ppermute | solution.py:298
  127.1 7.3 %collective-permute-done.10 = bf16[64,3072]{1,0:T(8,128)(2,1)S(1)} collective-permute-done((bf16[64,3072]{1,0:T(8,128)(2,1)S(1)}, bf16[64,3072]{1,0:T(8,128)(2,1)S(1)}, u32[]{:S(2)}, u32[]{:S(2)}) %collective-permute-start.10) | collective-permute-done | bytes 393248 | tf_op jit(solution)/shard_map/ppermute | solution.py:298
  (26 shorter events, 10.2 us)
Async XLA Ops:
  0.0 22.8 %collective-permute-start = (bf16[192,3072]{1,0:T(8,128)(2,1)}, bf16[192,3072]{1,0:T(8,128)(2,1)S(1)}, u32[]{:S(2)}, u32[]{:S(2)}) collective-permute-start(bf16[192,3072]{1,0:T(8,128)(2,1)} %bitcast.15), channel_id=1, source_target_pairs={{0,1},{1,0},{4,5},{5,4},{8,9},{9,8},{12,13},{13,12},{16,17},{17,16... | collective-permute-start | bytes 3538952 | tf_op jit(solution)/shard_map/ppermute | solution.py:301
  3.5 19.4 %copy-start.1 = (s32[64]{0:T(128)S(1)}, s32[64]{0:T(128)}, u32[]{:S(2)}) copy-start(s32[64]{0:T(128)} %patch_index.5) | copy-start | bytes 772
  12.3 1.4 %collective-permute-start.1 = (bf16[96,3072]{1,0:T(8,128)(2,1)S(1)}, bf16[96,3072]{1,0:T(8,128)(2,1)S(1)}, u32[]{:S(2)}, u32[]{:S(2)}) collective-permute-start(bf16[96,3072]{1,0:T(8,128)(2,1)S(1)} %get-tuple-element.33), channel_id=1, source_target_pairs={{2,3},{3,2},{6,7},{7,6},{10,11},{11,10},{14,15},{15,14},{18,19},{1... | collective-permute-start | bytes 1769480 | tf_op jit(solution)/shard_map/ppermute | solution.py:306
  13.0 0.7 collective-permute-start.2
  22.8 4.4 %copy-start = (s32[4]{0:T(128)S(1)}, s32[4]{0:T(128)}, u32[]{:S(2)}) copy-start(s32[4]{0:T(128)} %counts.11) | copy-start | bytes 52
  31.2 11.5 %collective-permute-start.6 = (bf16[96,3072]{1,0:T(8,128)(2,1)S(1)}, bf16[96,3072]{1,0:T(8,128)(2,1)S(1)}, u32[]{:S(2)}, u32[]{:S(2)}) collective-permute-start(bf16[96,3072]{1,0:T(8,128)(2,1)S(1)} %attend.8), channel_id=1, source_target_pairs={{0,1},{1,0},{2,3},{3,2},{4,5},{5,4},{6,7},{7,6},{8,9},{9,8},{10,11... | collective-permute-start | bytes 1769480 | tf_op jit(solution)/shard_map/ppermute | solution.py:295
  36.9 17.2 %collective-permute-start.3 = (bf16[96,3072]{1,0:T(8,128)(2,1)S(1)}, bf16[96,3072]{1,0:T(8,128)(2,1)S(1)}, u32[]{:S(2)}, u32[]{:S(2)}) collective-permute-start(bf16[96,3072]{1,0:T(8,128)(2,1)S(1)} %attend.7), channel_id=1, source_target_pairs={{0,1},{1,0},{2,3},{3,2},{4,5},{5,4},{6,7},{7,6},{8,9},{9,8},{10,11... | collective-permute-start | bytes 1769480 | tf_op jit(solution)/shard_map/ppermute | solution.py:295
  42.9 27.0 %collective-permute-start.7 = (bf16[96,3072]{1,0:T(8,128)(2,1)S(1)}, bf16[96,3072]{1,0:T(8,128)(2,1)S(1)}, u32[]{:S(2)}, u32[]{:S(2)}) collective-permute-start(bf16[96,3072]{1,0:T(8,128)(2,1)S(1)} %combine.6), channel_id=1, source_target_pairs={{0,2},{1,3},{2,5},{3,4},{4,6},{5,7},{6,9},{7,8},{8,10},{9,11},{10,... | collective-permute-start | bytes 1769480 | tf_op jit(solution)/shard_map/ppermute | solution.py:298
  54.3 22.2 %collective-permute-start.4 = (bf16[96,3072]{1,0:T(8,128)(2,1)S(1)}, bf16[96,3072]{1,0:T(8,128)(2,1)S(1)}, u32[]{:S(2)}, u32[]{:S(2)}) collective-permute-start(bf16[96,3072]{1,0:T(8,128)(2,1)S(1)} %combine.5), channel_id=1, source_target_pairs={{0,2},{1,3},{2,5},{3,4},{4,6},{5,7},{6,9},{7,8},{8,10},{9,11},{10,... | collective-permute-start | bytes 1769480 | tf_op jit(solution)/shard_map/ppermute | solution.py:298
  69.9 12.6 %collective-permute-start.8 = (bf16[96,3072]{1,0:T(8,128)(2,1)S(1)}, bf16[96,3072]{1,0:T(8,128)(2,1)S(1)}, u32[]{:S(2)}, u32[]{:S(2)}) collective-permute-start(bf16[96,3072]{1,0:T(8,128)(2,1)S(1)} %collective-permute-done.7.refs_1_), channel_id=1, source_target_pairs={{0,1},{1,0},{2,3},{3,2},{4,5},{5,4},{6,7},{7,6},{8,9},{9,8},{10,11... | collective-permute-start | bytes 1769480 | tf_op jit(solution)/shard_map/ppermute | solution.py:295
  76.5 12.3 %collective-permute-start.5 = (bf16[96,3072]{1,0:T(8,128)(2,1)S(1)}, bf16[96,3072]{1,0:T(8,128)(2,1)S(1)}, u32[]{:S(2)}, u32[]{:S(2)}) collective-permute-start(bf16[96,3072]{1,0:T(8,128)(2,1)S(1)} %collective-permute-done.4.refs_0_), channel_id=1, source_target_pairs={{0,1},{1,0},{2,3},{3,2},{4,5},{5,4},{6,7},{7,6},{8,9},{9,8},{10,11... | collective-permute-start | bytes 1769480 | tf_op jit(solution)/shard_map/ppermute | solution.py:295
  97.0 13.1 %collective-permute-start.11 = (bf16[64,3072]{1,0:T(8,128)(2,1)S(1)}, bf16[64,3072]{1,0:T(8,128)(2,1)S(1)}, u32[]{:S(2)}, u32[]{:S(2)}) collective-permute-start(bf16[64,3072]{1,0:T(8,128)(2,1)S(1)} %get-tuple-element.56), channel_id=1, source_target_pairs={{0,1},{1,0},{2,3},{3,2},{4,5},{5,4},{6,7},{7,6},{8,9},{9,8},{10,11... | collective-permute-start | bytes 1179656 | tf_op jit(solution)/shard_map/ppermute | solution.py:295
  98.5 13.2 %collective-permute-start.13 = (bf16[64,3072]{1,0:T(8,128)(2,1)S(1)}, bf16[64,3072]{1,0:T(8,128)(2,1)S(1)}, u32[]{:S(2)}, u32[]{:S(2)}) collective-permute-start(bf16[64,3072]{1,0:T(8,128)(2,1)S(1)} %get-tuple-element.58), channel_id=1, source_target_pairs={{0,1},{1,0},{2,3},{3,2},{4,5},{5,4},{6,7},{7,6},{8,9},{9,8},{10,11... | collective-permute-start | bytes 1179656 | tf_op jit(solution)/shard_map/ppermute | solution.py:295
  103.2 12.8 %collective-permute-start.9 = (bf16[64,3072]{1,0:T(8,128)(2,1)S(1)}, bf16[64,3072]{1,0:T(8,128)(2,1)S(1)}, u32[]{:S(2)}, u32[]{:S(2)}) collective-permute-start(bf16[64,3072]{1,0:T(8,128)(2,1)S(1)} %attend.10), channel_id=1, source_target_pairs={{0,1},{1,0},{2,3},{3,2},{4,5},{5,4},{6,7},{7,6},{8,9},{9,8},{10,11... | collective-permute-start | bytes 1179656 | tf_op jit(solution)/shard_map/ppermute | solution.py:295
  110.2 12.7 %collective-permute-start.12 = (bf16[64,3072]{1,0:T(8,128)(2,1)S(1)}, bf16[64,3072]{1,0:T(8,128)(2,1)S(1)}, u32[]{:S(2)}, u32[]{:S(2)}) collective-permute-start(bf16[64,3072]{1,0:T(8,128)(2,1)S(1)} %combine.8), channel_id=1, source_target_pairs={{0,2},{1,3},{2,5},{3,4},{4,6},{5,7},{6,9},{7,8},{8,10},{9,11},{10,... | collective-permute-start | bytes 1179656 | tf_op jit(solution)/shard_map/ppermute | solution.py:298
  111.9 15.2 %collective-permute-start.14 = (bf16[64,3072]{1,0:T(8,128)(2,1)S(1)}, bf16[64,3072]{1,0:T(8,128)(2,1)S(1)}, u32[]{:S(2)}, u32[]{:S(2)}) collective-permute-start(bf16[64,3072]{1,0:T(8,128)(2,1)S(1)} %combine.9), channel_id=1, source_target_pairs={{0,2},{1,3},{2,5},{3,4},{4,6},{5,7},{6,9},{7,8},{8,10},{9,11},{10,... | collective-permute-start | bytes 1179656 | tf_op jit(solution)/shard_map/ppermute | solution.py:298
  116.1 18.3 %collective-permute-start.10 = (bf16[64,3072]{1,0:T(8,128)(2,1)S(1)}, bf16[64,3072]{1,0:T(8,128)(2,1)S(1)}, u32[]{:S(2)}, u32[]{:S(2)}) collective-permute-start(bf16[64,3072]{1,0:T(8,128)(2,1)S(1)} %combine.7), channel_id=1, source_target_pairs={{0,2},{1,3},{2,5},{3,4},{4,6},{5,7},{6,9},{7,8},{8,10},{9,11},{10,... | collective-permute-start | bytes 1179656 | tf_op jit(solution)/shard_map/ppermute | solution.py:298
where the time goes:
time: 136 us
  waiting for transfers between devices  51.2 us (38%)
  Pallas kernels  48.7 us (36%)
  starting transfers between devices  34.4 us (25%)
    ppermute x5, waiting for transfers between devices, move(): return lax.ppermute(block, both, shift)  29.5 us
    pallas_call x6, Pallas kernels, attend(): pl.pallas_call(kernel, in_specs=[SMEM] + [VMEM] * (4 + len(extra)), out_s...  26.2 us
    ppermute x5, starting transfers between devices, move(): return lax.ppermute(block, both, shift)  22.8 us
    pallas_call x3, Pallas kernels, qkv(): pl.pallas_call(kernel, in_specs=[SMEM] + [VMEM] * (n + 5), out_specs=[VME...  13.1 us
    ppermute x7, waiting for transfers between devices, exchange(): return lax.ppermute(block, both, swap)  12.6 us
    ppermute x1, waiting for transfers between devices, on_device(): early = lax.ppermute(own, both, [p for p in swap if p[0] // 2 % 2 == 0])  9.14 us
    pallas_call x1, Pallas kernels, opening(): pl.pallas_call(open_kernel, in_specs=[HBM] * 9, out_specs=[VMEM] * 11, ou...  8.77 us
    ppermute x7, starting transfers between devices, exchange(): return lax.ppermute(block, both, swap)  6.67 us
  transfers between devices with their start and end apart: 15, of which 10 were waited for; matrix products, arithmetic and copies ran while one was open for 0% of the time, Pallas kernels for 24%

commit v1 on v0

--- a/solution.py
+++ b/solution.py
@@ -15,11 +15,12 @@
 VMEM = pl.BlockSpec(memory_space=pltpu.VMEM)
 SMEM = pl.BlockSpec(memory_space=pltpu.SMEM)
 HBM = pl.BlockSpec(memory_space=pltpu.HBM)
+LOOSE = pl.BlockSpec(memory_space=pl.ANY)
 MIB = 1024 * 1024
 QUERY_SCALE = HD ** (-0.5) * 1.4426950408889634
 BLOCK = 1536
 MID = (96, 96)
-LAST = (64, 64, 64)
+LAST = (80, 64, 48)
 
 
 def held(array):
@@ -171,7 +172,7 @@
     )(*map(far, (patch_index, step_index, rows, modulation, gains, w_qkv, w_out, keys, values)))
 
 
-def qkv(tick, side, patch_index, pairs, mods, gains, w_qkv, keys, values):
+def qkv(tick, side, patch_index, half, offset, pairs, mods, gains, w_qkv, keys, values, late=False):
     count, width = sum(p[0].shape[0] for p in pairs), keys.shape[1]
     n = sum(map(len, pairs))
 
@@ -184,27 +185,45 @@
             rows.append(one + jnp.concatenate(two, axis=0) if two else one)
             place += len(p)
         hidden = modulated(rows[0] if len(pairs) == 1 else jnp.concatenate(rows, axis=0), mods[...])
-        here = pl.ds(first_row(tick, side, patch_index, count), count)
-
-        def put_key(fresh):
-            keys[here, :] = fresh
-
-        def put_value(fresh):
-            values[here, :] = fresh
-
-        none = [lambda: None] * 3
-        projections(hidden, gains[...], w_qkv, none, put_key, put_value, query)
+        here = pl.ds(pl.multiple_of(first_row(tick, side, patch_index, half) + offset, 32), count)
+        if late:
+            query[...] = hidden
+        keys[here, :] = head_norm(project(hidden, w_qkv[1]), gains[1:2])
+        values[here, :] = project(hidden, w_qkv[2]).astype(BF16)
+        if not late:
+            query[...] = head_norm(project(hidden, w_qkv[0]), gains[0:1] * QUERY_SCALE)
 
     return pl.pallas_call(
         kernel,
         in_specs=[SMEM] + [VMEM] * (n + 5),
         out_specs=[VMEM] * 3,
-        out_shape=[in_vmem((count, width), BF16), in_vmem(keys.shape, BF16), in_vmem(values.shape, BF16)],
+        out_shape=[
+            in_vmem((count, pairs[0][0].shape[1] if late else width), BF16),
+            in_vmem(keys.shape, BF16),
+            in_vmem(values.shape, BF16),
+        ],
         input_output_aliases={n + 4: 1, n + 5: 2},
         compiler_params=limit(16),
         cost_estimate=cost(2 * w_qkv.size * 256),
         name="qkv",
     )(patch_index, *(a for p in pairs for a in p), mods, gains, held(w_qkv), held(keys), held(values))
+
+
+def late_query_kernel(hidden, gains, w_qkv, after, query):
+    del after
+    query[...] = head_norm(project(hidden[...], w_qkv[0]), gains[0:1] * QUERY_SCALE)
+
+
+def late_query(hidden, gains, w_qkv, after):
+    return pl.pallas_call(
+        late_query_kernel,
+        in_specs=[VMEM] * 3 + [LOOSE],
+        out_specs=VMEM,
+        out_shape=in_vmem((hidden.shape[0], w_qkv.shape[2]), BF16),
+        compiler_params=limit(16),
+        cost_estimate=cost(2 * w_qkv.size * 256 / 3),
+        name="late_query",
+    )(held(hidden), gains, held(w_qkv), after)
 
 
 def attended(query, keys, values, counts):
@@ -232,11 +251,17 @@
 def attend(begin, sizes, counts, query, keys, values, w_out, pieces=(), mods=None):
     count, model = sum(sizes), w_out.shape[1]
     keep = len(pieces) > 0
-    n = len(pieces)
-
-    def kernel(counts, query, keys, values, w_out, *refs):
+    queries = query if isinstance(query, tuple) else (query,)
+    n, k = len(pieces), len(queries)
+
+    def kernel(counts, *refs):
+        query, (keys, values, w_out), refs = refs[:k], refs[k : k + 3], refs[k + 3 :]
         out, outs = refs[-1], refs[-1 - len(sizes) : -1]
-        out[...] = attended(query[begin : begin + count, :], keys, values, counts)
+        if k == 1:
+            rows = query[0][begin : begin + count, :]
+        else:
+            rows = jnp.concatenate([q[...] for q in query], axis=0)
+        out[...] = attended(rows, keys, values, counts)
 
         def columns(i, carry):
             cols = pl.ds(pl.multiple_of(i * BLOCK, BLOCK), BLOCK)
@@ -255,14 +280,14 @@
     extra = (*pieces, mods) if keep else ()
     return pl.pallas_call(
         kernel,
-        in_specs=[SMEM] + [VMEM] * (4 + len(extra)),
+        in_specs=[SMEM] + [VMEM] * (3 + k + len(extra)),
         out_specs=[VMEM] * len(sizes),
         out_shape=[in_vmem((size, model), F32 if keep else BF16) for size in sizes],
-        scratch_shapes=[pltpu.VMEM((count, query.shape[1]), BF16)],
+        scratch_shapes=[pltpu.VMEM((count, keys.shape[1]), BF16)],
         compiler_params=limit(16),
-        cost_estimate=cost(2 * 256 * query.shape[1] * (2 * keys.shape[0] + model)),
+        cost_estimate=cost(2 * 256 * keys.shape[1] * (2 * keys.shape[0] + model)),
         name="attend",
-    )(counts, held(query), held(keys), held(values), held(w_out), *extra)
+    )(counts, *map(held, queries), held(keys), held(values), held(w_out), *extra)
 
 
 def combine_kernel(base, received, mods, out):
@@ -305,7 +330,7 @@
     )
     late = [lax.ppermute(piece, both, [p for p in swap if p[0] // 2 % 2 == 1]) for piece in (upper, lower)]
     query_other, keys, values = qkv(
-        0, 1, patch_index, [(early, *late)], mods, gains, weights, keys, values
+        0, 1, patch_index, own.shape[0], 0, [(early, *late)], mods, gains, weights, keys, values
     )
     begin = 0
     got = []
@@ -317,12 +342,19 @@
 
     mods = mods_next
     other = [exchange(block) for block in own]
-    query, keys, values = qkv(1, 0, patch_index, [(p,) for p in own], mods, gains, weights, keys, values)
-    query_other, keys, values = qkv(1, 1, patch_index, [(p,) for p in other], mods, gains, weights, keys, values)
+    half = patches.shape[1]
+    query, keys, values = qkv(1, 0, patch_index, half, 0, [(p,) for p in own], mods, gains, weights, keys, values)
+    query_other, keys, values = qkv(
+        1, 1, patch_index, half, 0, [(other[0],)], mods, gains, weights, keys, values
+    )
+    hidden, keys, values = qkv(
+        1, 1, patch_index, half, MID[0], [(other[1],)], mods, gains, weights, keys, values, late=True
+    )
     one = attend(0, LAST[:1], counts, query, keys, values, proj)
     two = attend(LAST[0], LAST[1:], counts, query, keys, values, proj)
     got = [exchange(block) for block in (*one, *two)]
-    base = attend(0, LAST, counts, query_other, keys, values, proj, other, mods)
+    rest = late_query(hidden, gains, weights, two[0])
+    base = attend(0, LAST, counts, (query_other, rest), keys, values, proj, other, mods)
     done = [move(combine(b, g, mods)) for b, g in zip(base, got)]
     return jnp.concatenate(done, axis=0)[None]
 

time: 136 us -> 133 us (0.978)
  waiting for transfers between devices: 51.2 us -> 43.9 us
  Pallas kernels: 48.7 us -> 51.4 us
  starting transfers between devices: 34.4 us -> 36.4 us
    ppermute x7, waiting for transfers between devices: 12.6 us -> 8.34 us  [exchange(): return lax.ppermute(block, both, swap)]
    ppermute x5, waiting for transfers between devices: 29.5 us -> 26.4 us  [move(): return lax.ppermute(block, both, shift)]
    ppermute x5, starting transfers between devices: 22.8 us -> 24.8 us  [move(): return lax.ppermute(block, both, shift)]
    pallas_call x3 -> x4, Pallas kernels: 13.1 us -> 14.7 us  [qkv(): pl.pallas_call(kernel, in_specs=[SMEM] + [VMEM] * (n + 5), out_specs=[VME...]
    pallas_call x6 -> x7, Pallas kernels: 26.2 us -> 27.2 us  [the longest x6 26.2 us: attend(): pl.pallas_call(kernel, in_specs=[SMEM] + [VMEM] * (3 + k + len(extra)), o...]
  transfers between devices with their start and end apart: 15 -> 15, of which waited for: 10 -> 8; matrix products, arithmetic and copies ran while one was open for 0% -> 0% of each run, Pallas kernels for 24% -> 27%
where the time goes in v1:
time: 133 us
  Pallas kernels  51.4 us (39%)
  waiting for transfers between devices  43.9 us (33%)
  starting transfers between devices  36.4 us (27%)
    ppermute x5, waiting for transfers between devices, move(): return lax.ppermute(block, both, shift)  26.4 us
    pallas_call x6, Pallas kernels, attend(): pl.pallas_call(kernel, in_specs=[SMEM] + [VMEM] * (3 + k + len(extra)), o...  26.2 us
    ppermute x5, starting transfers between devices, move(): return lax.ppermute(block, both, shift)  24.8 us
    pallas_call x4, Pallas kernels, qkv(): pl.pallas_call(kernel, in_specs=[SMEM] + [VMEM] * (n + 5), out_specs=[VME...  14.7 us
    ppermute x1, waiting for transfers between devices, on_device(): early = lax.ppermute(own, both, [p for p in swap if p[0] // 2 % 2 == 0])  9.14 us
    pallas_call x1, Pallas kernels, opening(): pl.pallas_call(open_kernel, in_specs=[HBM] * 9, out_specs=[VMEM] * 11, ou...  8.77 us
    ppermute x7, waiting for transfers between devices, exchange(): return lax.ppermute(block, both, swap)  8.34 us
    ppermute x7, starting transfers between devices, exchange(): return lax.ppermute(block, both, swap)  6.76 us
  transfers between devices with their start and end apart: 15, of which 8 were waited for; matrix products, arithmetic and copies ran while one was open for 0% of the time, Pallas kernels for 27%

profile of v1, /device:TPU:0, one launch (start us, length us, event | category | flops | bytes accessed | tf_op | source)
XLA Modules:
  0.0 132.9 jit_solution(11747205563598803095)
XLA Ops:
  0.0 3.5 %collective-permute-start = (bf16[192,3072]{1,0:T(8,128)(2,1)}, bf16[192,3072]{1,0:T(8,128)(2,1)S(1)}, u32[]{:S(2)}, u32[]{:S(2)}) collective-permute-start(bf16[192,3072]{1,0:T(8,128)(2,1)} %bitcast.15), channel_id=1, source_target_pairs={{0,1},{1,0},{4,5},{5,4},{8,9},{9,8},{12,13},{13,12},{16,17},{17,16... | collective-permute-start | bytes 3538952 | tf_op jit(solution)/shard_map/ppermute | solution.py:326
  3.5 8.8 %opening.1 = (bf16[192,768]{1,0:T(8,128)(2,1)S(1)}, bf16[192,3072]{1,0:T(8,128)(2,1)S(1)}, bf16[96,3072]{1,0:T(8,128)(2,1)S(1)}, bf16[96,3072]{1,0:T(8,128)(2,1)...) custom-call(s32[64]{0:T(128)} %patch_index.7, ...), custom_call_target="tpu_custom_call" | custom-call | flops 3623878656 | bytes 1000000 | tf_op jit(solution)/shard_map/opening/pallas_call | solution.py:145
  13.7 9.1 %collective-permute-done.refs_0_ = bf16[192,3072]{1,0:T(8,128)(2,1)S(1)} collective-permute-done((bf16[192,3072]{1,0:T(8,128)(2,1)}, bf16[192,3072]{1,0:T(8,128)(2,1)S(1)}, u32[]{:S(2)}, u32[]{:S(2)}) %collective-permute-start) | collective-permute-done | bytes 1179680 | tf_op jit(solution)/shard_map/ppermute | solution.py:326
  22.8 4.4 %qkv.4 = (bf16[192,768]{1,0:T(8,128)(2,1)S(1)}, bf16[1792,768]{1,0:T(8,128)(2,1)S(1)}, bf16[1792,768]{1,0:T(8,128)(2,1)S(1)}) custom-call(s32[64]{0:T(128)S(1)} %copy-done.1, bf16[192,3072]{1,0:T(8,128)(2,1)S(1)} %collective-permute-done.refs_0_, bf16[96,3072]{1,0:T(8,128)(2,1)S(1)} %collective-permute-done.1.refs_1_, ...), custom_call_target="tpu_custom_call", output_to_operand_aliasing={{1}: (7, {}), {2}: (8, {})} | custom-call | flops 3623878656 | bytes 1000000 | tf_op jit(solution)/shard_map/qkv/pallas_call | solution.py:196
  27.2 4.0 %attend.7 = bf16[96,3072]{1,0:T(8,128)(2,1)S(1)} custom-call(s32[4]{0:T(128)S(1)} %copy-done, bf16[192,768]{1,0:T(8,128)(2,1)S(1)} %get-tuple-element.48.refs_0_, bf16[1792,768]{1,0:T(8,128)(2,1)S(1)} %get-tuple-element.43.refs_1_.refs_5_, bf16[1792,768]{1,0:T(8,128)(2,1)S(1)} %get-tuple-element.44.refs_2_.refs_6_, ...), custom_call_target="tpu_custom_call" | custom-call | flops 2617245696 | bytes 1000000 | tf_op jit(solution)/shard_map/attend/pallas_call | solution.py:281
  31.2 1.7 %collective-permute-start.3 = (bf16[96,3072]{1,0:T(8,128)(2,1)S(1)}, bf16[96,3072]{1,0:T(8,128)(2,1)S(1)}, u32[]{:S(2)}, u32[]{:S(2)}) collective-permute-start(bf16[96,3072]{1,0:T(8,128)(2,1)S(1)} %attend.7), channel_id=1, source_target_pairs={{0,1},{1,0},{2,3},{3,2},{4,5},{5,4},{6,7},{7,6},{8,9},{9,8},{10,11... | collective-permute-start | bytes 1769480 | tf_op jit(solution)/shard_map/ppermute | solution.py:320
  32.9 4.0 %attend.8 = bf16[96,3072]{1,0:T(8,128)(2,1)S(1)} custom-call(s32[4]{0:T(128)S(1)} %copy-done, bf16[192,768]{1,0:T(8,128)(2,1)S(1)} %get-tuple-element.48.refs_0_, bf16[1792,768]{1,0:T(8,128)(2,1)S(1)} %get-tuple-element.43.refs_1_.refs_5_, bf16[1792,768]{1,0:T(8,128)(2,1)S(1)} %get-tuple-element.44.refs_2_.refs_6_, ...), custom_call_target="tpu_custom_call" | custom-call | flops 2617245696 | bytes 1000000 | tf_op jit(solution)/shard_map/attend/pallas_call | solution.py:281
  37.6 5.1 %attend.6 = (f32[96,3072]{1,0:T(8,128)S(1)}, f32[96,3072]{1,0:T(8,128)S(1)}) custom-call(s32[4]{0:T(128)S(1)} %copy-done, bf16[192,768]{1,0:T(8,128)(2,1)S(1)} %get-tuple-element.35.refs_0_, bf16[1792,768]{1,0:T(8,128)(2,1)S(1)} %get-tuple-element.43.refs_1_.refs_5_, bf16[1792,768]{1,0:T(8,128)(2,1)S(1)} %get-tuple-element.44.refs_2_.refs_6_, ...), custom_call_target="tpu_custom_call" | custom-call | flops 2617245696 | bytes 1000000 | tf_op jit(solution)/shard_map/attend/pallas_call | solution.py:281
  42.9 11.2 %collective-permute-start.4 = (bf16[96,3072]{1,0:T(8,128)(2,1)S(1)}, bf16[96,3072]{1,0:T(8,128)(2,1)S(1)}, u32[]{:S(2)}, u32[]{:S(2)}) collective-permute-start(bf16[96,3072]{1,0:T(8,128)(2,1)S(1)} %combine.5), channel_id=1, source_target_pairs={{0,2},{1,3},{2,5},{3,4},{4,6},{5,7},{6,9},{7,8},{8,10},{9,11},{10,... | collective-permute-start | bytes 1769480 | tf_op jit(solution)/shard_map/ppermute | solution.py:323
  54.3 6.1 %collective-permute-start.7 = (bf16[96,3072]{1,0:T(8,128)(2,1)S(1)}, bf16[96,3072]{1,0:T(8,128)(2,1)S(1)}, u32[]{:S(2)}, u32[]{:S(2)}) collective-permute-start(bf16[96,3072]{1,0:T(8,128)(2,1)S(1)} %combine.6), channel_id=1, source_target_pairs={{0,2},{1,3},{2,5},{3,4},{4,6},{5,7},{6,9},{7,8},{8,10},{9,11},{10,... | collective-permute-start | bytes 1769480 | tf_op jit(solution)/shard_map/ppermute | solution.py:323
  60.4 9.5 %collective-permute-done.4.refs_0_ = bf16[96,3072]{1,0:T(8,128)(2,1)S(1)} collective-permute-done((bf16[96,3072]{1,0:T(8,128)(2,1)S(1)}, bf16[96,3072]{1,0:T(8,128)(2,1)S(1)}, u32[]{:S(2)}, u32[]{:S(2)}) %collective-permute-start.4) | collective-permute-done | bytes 589856 | tf_op jit(solution)/shard_map/ppermute | solution.py:323
  70.1 6.4 %collective-permute-done.7.refs_1_ = bf16[96,3072]{1,0:T(8,128)(2,1)S(1)} collective-permute-done((bf16[96,3072]{1,0:T(8,128)(2,1)S(1)}, bf16[96,3072]{1,0:T(8,128)(2,1)S(1)}, u32[]{:S(2)}, u32[]{:S(2)}) %collective-permute-start.7) | collective-permute-done | bytes 589856 | tf_op jit(solution)/shard_map/ppermute | solution.py:323
  76.7 4.3 %qkv.5 = (bf16[192,768]{1,0:T(8,128)(2,1)S(1)}, bf16[1792,768]{1,0:T(8,128)(2,1)S(1)}, bf16[1792,768]{1,0:T(8,128)(2,1)S(1)}) custom-call(s32[64]{0:T(128)S(1)} %copy-done.1, bf16[96,3072]{1,0:T(8,128)(2,1)S(1)} %collective-permute-done.4.refs_0_, bf16[96,3072]{1,0:T(8,128)(2,1)S(1)} %collective-permute-done.7.refs_1_, ...), custom_call_target="tpu_custom_call", output_to_operand_aliasing={{1}: (6, {}), {2}: (7, {})} | custom-call | flops 3623878656 | bytes 1000000 | tf_op jit(solution)/shard_map/qkv/pallas_call | solution.py:196
  82.5 3.4 %qkv.6 = (bf16[96,768]{1,0:T(8,128)(2,1)S(1)}, bf16[1792,768]{1,0:T(8,128)(2,1)S(1)}, bf16[1792,768]{1,0:T(8,128)(2,1)S(1)}) custom-call(s32[64]{0:T(128)S(1)} %copy-done.1, bf16[96,3072]{1,0:T(8,128)(2,1)S(1)} %collective-permute-done.5.refs_0_.refs_5_, ...), custom_call_target="tpu_custom_call", output_to_operand_aliasing={{1}: (5, {}), {2}: (6, {})} | custom-call | flops 3623878656 | bytes 1000000 | tf_op jit(solution)/shard_map/qkv/pallas_call | solution.py:196
  85.9 2.9 %collective-permute-done.8.refs_0_.refs_6_ = bf16[96,3072]{1,0:T(8,128)(2,1)S(1)} collective-permute-done((bf16[96,3072]{1,0:T(8,128)(2,1)S(1)}, bf16[96,3072]{1,0:T(8,128)(2,1)S(1)}, u32[]{:S(2)}, u32[]{:S(2)}) %collective-permute-start.8) | collective-permute-done | bytes 589856 | tf_op jit(solution)/shard_map/ppermute | solution.py:320
  88.8 2.6 %qkv.7 = (bf16[96,3072]{1,0:T(8,128)(2,1)S(1)}, bf16[1792,768]{1,0:T(8,128)(2,1)S(1)}, bf16[1792,768]{1,0:T(8,128)(2,1)S(1)}) custom-call(s32[64]{0:T(128)S(1)} %copy-done.1, bf16[96,3072]{1,0:T(8,128)(2,1)S(1)} %collective-permute-done.8.refs_0_.refs_6_, ...), custom_call_target="tpu_custom_call", output_to_operand_aliasing={{1}: (5, {}), {2}: (6, {})} | custom-call | flops 3623878656 | bytes 1000000 | tf_op jit(solution)/shard_map/qkv/pallas_call | solution.py:196
  91.4 4.1 %attend.11 = bf16[80,3072]{1,0:T(8,128)(2,1)S(1)} custom-call(s32[4]{0:T(128)S(1)} %copy-done, bf16[192,768]{1,0:T(8,128)(2,1)S(1)} %get-tuple-element.57.refs_0_, bf16[1792,768]{1,0:T(8,128)(2,1)S(1)} %get-tuple-element.58.refs_1_.refs_2_, bf16[1792,768]{1,0:T(8,128)(2,1)S(1)} %get-tuple-element.59.refs_2_.refs_3_, ...), custom_call_target="tpu_custom_call" | custom-call | flops 2617245696 | bytes 1000000 | tf_op jit(solution)/shard_map/attend/pallas_call | solution.py:281
  97.0 3.9 %attend.9 = (bf16[64,3072]{1,0:T(8,128)(2,1)S(1)}, bf16[48,3072]{1,0:T(8,128)(2,1)S(1)}) custom-call(s32[4]{0:T(128)S(1)} %copy-done, bf16[192,768]{1,0:T(8,128)(2,1)S(1)} %get-tuple-element.57.refs_0_, bf16[1792,768]{1,0:T(8,128)(2,1)S(1)} %get-tuple-element.58.refs_1_.refs_2_, bf16[1792,768]{1,0:T(8,128)(2,1)S(1)} %get-tuple-element.59.refs_2_.refs_3_, ...), custom_call_target="tpu_custom_call" | custom-call | flops 2617245696 | bytes 1000000 | tf_op jit(solution)/shard_map/attend/pallas_call | solution.py:281
  102.8 1.5 %collective-permute-start.13 = (bf16[48,3072]{1,0:T(8,128)(2,1)S(1)}, bf16[48,3072]{1,0:T(8,128)(2,1)S(1)}, u32[]{:S(2)}, u32[]{:S(2)}) collective-permute-start(bf16[48,3072]{1,0:T(8,128)(2,1)S(1)} %get-tuple-element.64), channel_id=1, source_target_pairs={{0,1},{1,0},{2,3},{3,2},{4,5},{5,4},{6,7},{7,6},{8,9},{9,8},{10,11... | collective-permute-start | bytes 884744 | tf_op jit(solution)/shard_map/ppermute | solution.py:320
  104.3 5.1 %attend.10 = (f32[80,3072]{1,0:T(8,128)S(1)}, f32[64,3072]{1,0:T(8,128)S(1)}, f32[48,3072]{1,0:T(8,128)S(1)}) custom-call(s32[4]{0:T(128)S(1)} %copy-done, bf16[96,768]{1,0:T(8,128)(2,1)S(1)} %get-tuple-element.53.refs_0_, bf16[96,768]{1,0:T(8,128)(2,1)S(1)} %late_query.1.refs_1_, bf16[1792,768]{1,0:T(8,128)(2,1)S(1)} %get-tuple-element.58.refs_1_.refs_2_, ...), custom_call_target="tpu_custom_call" | custom-call | flops 2617245696 | bytes 1000000 | tf_op jit(solution)/shard_map/attend/pallas_call | solution.py:281
  109.7 2.0 %collective-permute-done.11.received = bf16[64,3072]{1,0:T(8,128)(2,1)S(1)} collective-permute-done((bf16[64,3072]{1,0:T(8,128)(2,1)S(1)}, bf16[64,3072]{1,0:T(8,128)(2,1)S(1)}, u32[]{:S(2)}, u32[]{:S(2)}) %collective-permute-start.11) | collective-permute-done | bytes 393248 | tf_op jit(solution)/shard_map/ppermute | solution.py:320
  112.9 2.0 %collective-permute-done.13.received = bf16[48,3072]{1,0:T(8,128)(2,1)S(1)} collective-permute-done((bf16[48,3072]{1,0:T(8,128)(2,1)S(1)}, bf16[48,3072]{1,0:T(8,128)(2,1)S(1)}, u32[]{:S(2)}, u32[]{:S(2)}) %collective-permute-start.13) | collective-permute-done | bytes 294944 | tf_op jit(solution)/shard_map/ppermute | solution.py:320
  115.0 6.3 %collective-permute-start.14 = (bf16[48,3072]{1,0:T(8,128)(2,1)S(1)}, bf16[48,3072]{1,0:T(8,128)(2,1)S(1)}, u32[]{:S(2)}, u32[]{:S(2)}) collective-permute-start(bf16[48,3072]{1,0:T(8,128)(2,1)S(1)} %combine.9), channel_id=1, source_target_pairs={{0,2},{1,3},{2,5},{3,4},{4,6},{5,7},{6,9},{7,8},{8,10},{9,11},{10,... | collective-permute-start | bytes 884744 | tf_op jit(solution)/shard_map/ppermute | solution.py:323
  121.3 10.5 %collective-permute-done.14 = bf16[48,3072]{1,0:T(8,128)(2,1)S(1)} collective-permute-done((bf16[48,3072]{1,0:T(8,128)(2,1)S(1)}, bf16[48,3072]{1,0:T(8,128)(2,1)S(1)}, u32[]{:S(2)}, u32[]{:S(2)}) %collective-permute-start.14) | collective-permute-done | bytes 294944 | tf_op jit(solution)/shard_map/ppermute | solution.py:323
  (28 shorter events, 10.4 us)
Async XLA Ops:
  0.0 22.8 %collective-permute-start = (bf16[192,3072]{1,0:T(8,128)(2,1)}, bf16[192,3072]{1,0:T(8,128)(2,1)S(1)}, u32[]{:S(2)}, u32[]{:S(2)}) collective-permute-start(bf16[192,3072]{1,0:T(8,128)(2,1)} %bitcast.15), channel_id=1, source_target_pairs={{0,1},{1,0},{4,5},{5,4},{8,9},{9,8},{12,13},{13,12},{16,17},{17,16... | collective-permute-start | bytes 3538952 | tf_op jit(solution)/shard_map/ppermute | solution.py:326
  3.5 19.4 %copy-start.1 = (s32[64]{0:T(128)S(1)}, s32[64]{0:T(128)}, u32[]{:S(2)}) copy-start(s32[64]{0:T(128)} %patch_index.7) | copy-start | bytes 772
  12.3 1.4 %collective-permute-start.1 = (bf16[96,3072]{1,0:T(8,128)(2,1)S(1)}, bf16[96,3072]{1,0:T(8,128)(2,1)S(1)}, u32[]{:S(2)}, u32[]{:S(2)}) collective-permute-start(bf16[96,3072]{1,0:T(8,128)(2,1)S(1)} %get-tuple-element.36), channel_id=1, source_target_pairs={{2,3},{3,2},{6,7},{7,6},{10,11},{11,10},{14,15},{15,14},{18,19},{1... | collective-permute-start | bytes 1769480 | tf_op jit(solution)/shard_map/ppermute | solution.py:331
  13.0 0.7 collective-permute-start.2
  22.8 4.4 %copy-start = (s32[4]{0:T(128)S(1)}, s32[4]{0:T(128)}, u32[]{:S(2)}) copy-start(s32[4]{0:T(128)} %counts.11) | copy-start | bytes 52
  31.2 11.5 %collective-permute-start.3 = (bf16[96,3072]{1,0:T(8,128)(2,1)S(1)}, bf16[96,3072]{1,0:T(8,128)(2,1)S(1)}, u32[]{:S(2)}, u32[]{:S(2)}) collective-permute-start(bf16[96,3072]{1,0:T(8,128)(2,1)S(1)} %attend.7), channel_id=1, source_target_pairs={{0,1},{1,0},{2,3},{3,2},{4,5},{5,4},{6,7},{7,6},{8,9},{9,8},{10,11... | collective-permute-start | bytes 1769480 | tf_op jit(solution)/shard_map/ppermute | solution.py:320
  36.9 17.2 %collective-permute-start.6 = (bf16[96,3072]{1,0:T(8,128)(2,1)S(1)}, bf16[96,3072]{1,0:T(8,128)(2,1)S(1)}, u32[]{:S(2)}, u32[]{:S(2)}) collective-permute-start(bf16[96,3072]{1,0:T(8,128)(2,1)S(1)} %attend.8), channel_id=1, source_target_pairs={{0,1},{1,0},{2,3},{3,2},{4,5},{5,4},{6,7},{7,6},{8,9},{9,8},{10,11... | collective-permute-start | bytes 1769480 | tf_op jit(solution)/shard_map/ppermute | solution.py:320
  42.9 27.0 %collective-permute-start.4 = (bf16[96,3072]{1,0:T(8,128)(2,1)S(1)}, bf16[96,3072]{1,0:T(8,128)(2,1)S(1)}, u32[]{:S(2)}, u32[]{:S(2)}) collective-permute-start(bf16[96,3072]{1,0:T(8,128)(2,1)S(1)} %combine.5), channel_id=1, source_target_pairs={{0,2},{1,3},{2,5},{3,4},{4,6},{5,7},{6,9},{7,8},{8,10},{9,11},{10,... | collective-permute-start | bytes 1769480 | tf_op jit(solution)/shard_map/ppermute | solution.py:323
  54.3 22.2 %collective-permute-start.7 = (bf16[96,3072]{1,0:T(8,128)(2,1)S(1)}, bf16[96,3072]{1,0:T(8,128)(2,1)S(1)}, u32[]{:S(2)}, u32[]{:S(2)}) collective-permute-start(bf16[96,3072]{1,0:T(8,128)(2,1)S(1)} %combine.6), channel_id=1, source_target_pairs={{0,2},{1,3},{2,5},{3,4},{4,6},{5,7},{6,9},{7,8},{8,10},{9,11},{10,... | collective-permute-start | bytes 1769480 | tf_op jit(solution)/shard_map/ppermute | solution.py:323
  69.9 12.6 %collective-permute-start.5 = (bf16[96,3072]{1,0:T(8,128)(2,1)S(1)}, bf16[96,3072]{1,0:T(8,128)(2,1)S(1)}, u32[]{:S(2)}, u32[]{:S(2)}) collective-permute-start(bf16[96,3072]{1,0:T(8,128)(2,1)S(1)} %collective-permute-done.4.refs_0_), channel_id=1, source_target_pairs={{0,1},{1,0},{2,3},{3,2},{4,5},{5,4},{6,7},{7,6},{8,9},{9,8},{10,11... | collective-permute-start | bytes 1769480 | tf_op jit(solution)/shard_map/ppermute | solution.py:320
  76.5 12.3 %collective-permute-start.8 = (bf16[96,3072]{1,0:T(8,128)(2,1)S(1)}, bf16[96,3072]{1,0:T(8,128)(2,1)S(1)}, u32[]{:S(2)}, u32[]{:S(2)}) collective-permute-start(bf16[96,3072]{1,0:T(8,128)(2,1)S(1)} %collective-permute-done.7.refs_1_), channel_id=1, source_target_pairs={{0,1},{1,0},{2,3},{3,2},{4,5},{5,4},{6,7},{7,6},{8,9},{9,8},{10,11... | collective-permute-start | bytes 1769480 | tf_op jit(solution)/shard_map/ppermute | solution.py:320
  95.5 14.0 %collective-permute-start.9 = (bf16[80,3072]{1,0:T(8,128)(2,1)S(1)}, bf16[80,3072]{1,0:T(8,128)(2,1)S(1)}, u32[]{:S(2)}, u32[]{:S(2)}) collective-permute-start(bf16[80,3072]{1,0:T(8,128)(2,1)S(1)} %attend.11), channel_id=1, source_target_pairs={{0,1},{1,0},{2,3},{3,2},{4,5},{5,4},{6,7},{7,6},{8,9},{9,8},{10,11... | collective-permute-start | bytes 1474568 | tf_op jit(solution)/shard_map/ppermute | solution.py:320
  100.9 10.8 %collective-permute-start.11 = (bf16[64,3072]{1,0:T(8,128)(2,1)S(1)}, bf16[64,3072]{1,0:T(8,128)(2,1)S(1)}, u32[]{:S(2)}, u32[]{:S(2)}) collective-permute-start(bf16[64,3072]{1,0:T(8,128)(2,1)S(1)} %get-tuple-element.60.after), channel_id=1, source_target_pairs={{0,1},{1,0},{2,3},{3,2},{4,5},{5,4},{6,7},{7,6},{8,9},{9,8},{10,11... | collective-permute-start | bytes 1179656 | tf_op jit(solution)/shard_map/ppermute | solution.py:320
  102.8 12.0 %collective-permute-start.13 = (bf16[48,3072]{1,0:T(8,128)(2,1)S(1)}, bf16[48,3072]{1,0:T(8,128)(2,1)S(1)}, u32[]{:S(2)}, u32[]{:S(2)}) collective-permute-start(bf16[48,3072]{1,0:T(8,128)(2,1)S(1)} %get-tuple-element.64), channel_id=1, source_target_pairs={{0,1},{1,0},{2,3},{3,2},{4,5},{5,4},{6,7},{7,6},{8,9},{9,8},{10,11... | collective-permute-start | bytes 884744 | tf_op jit(solution)/shard_map/ppermute | solution.py:320
  109.6 22.2 %collective-permute-start.10 = (bf16[80,3072]{1,0:T(8,128)(2,1)S(1)}, bf16[80,3072]{1,0:T(8,128)(2,1)S(1)}, u32[]{:S(2)}, u32[]{:S(2)}) collective-permute-start(bf16[80,3072]{1,0:T(8,128)(2,1)S(1)} %combine.7), channel_id=1, source_target_pairs={{0,2},{1,3},{2,5},{3,4},{4,6},{5,7},{6,9},{7,8},{8,10},{9,11},{10,... | collective-permute-start | bytes 1474568 | tf_op jit(solution)/shard_map/ppermute | solution.py:323
  111.8 20.0 %collective-permute-start.12 = (bf16[64,3072]{1,0:T(8,128)(2,1)S(1)}, bf16[64,3072]{1,0:T(8,128)(2,1)S(1)}, u32[]{:S(2)}, u32[]{:S(2)}) collective-permute-start(bf16[64,3072]{1,0:T(8,128)(2,1)S(1)} %combine.8), channel_id=1, source_target_pairs={{0,2},{1,3},{2,5},{3,4},{4,6},{5,7},{6,9},{7,8},{8,10},{9,11},{10,... | collective-permute-start | bytes 1179656 | tf_op jit(solution)/shard_map/ppermute | solution.py:323
  115.0 16.8 %collective-permute-start.14 = (bf16[48,3072]{1,0:T(8,128)(2,1)S(1)}, bf16[48,3072]{1,0:T(8,128)(2,1)S(1)}, u32[]{:S(2)}, u32[]{:S(2)}) collective-permute-start(bf16[48,3072]{1,0:T(8,128)(2,1)S(1)} %combine.9), channel_id=1, source_target_pairs={{0,2},{1,3},{2,5},{3,4},{4,6},{5,7},{6,9},{7,8},{8,10},{9,11},{10,... | collective-permute-start | bytes 884744 | tf_op jit(solution)/shard_map/ppermute | solution.py:323
